TPU v7x, 32 devices: a whole 2x2x4 slice. The times are simulated.
32 devices in a mesh: series: 2 (over x), tm: 16 (over z, y, core).
Axes of the slice: x: 2, y: 2, z: 4, core: 2. Of those that a mesh axis runs over, the one named last changes fastest.
Arguments:
- y_obs: bfloat16 [8192, 8192], P('series', 'tm'), may hold values from -6 to 6
- tile_mask: int32 [64, 64], P('series', 'tm'), may hold values 0 or 1
- factors: float32 [8192, 128], P(('series', 'tm')), may hold values from -0.5 to 0.5
- adam_m: float32 [8192, 128], P(('series', 'tm')), may hold values from -3 to 3
- adam_v: float32 [8192, 128], P(('series', 'tm')), may hold values from 0.1 to 10
- basis: float32 [128, 8192], P('series', 'tm'), may hold values from -6 to 6
- dilations: int32 [4], replicated, may hold values from 1 to 32, as said below
- conv_w: bfloat16 [4, 2, 128, 128], replicated, may hold values from -0.375 to 0.375
- conv_b: float32 [4, 128], replicated, may hold values from -3 to 3
Outputs:
- factors_new: float32 [8192, 128], P(('series', 'tm'))
- m_new: float32 [8192, 128], P(('series', 'tm'))
- v_new: float32 [8192, 128], P(('series', 'tm'))
- basis_new: float32 [128, 8192], P('series', 'tm')
Inputs may be any that keep to these rules, and one draw needn't show every extreme that they name: `dilations`: at least one layer has dilation 32.
All inputs are finite; a program needn't handle non-finite values. No bound on the sum of `tile_mask` on one device may be relied on, other than what follows from the above.
Results may differ from a plain program's by a relative error of at most 0.0031.
Values may be sent and summed in bfloat16 or wider, within the bound.
A program may use at most 64 MiB of HBM per device.

v0:
```python
import functools
import math

import jax
import jax.numpy as jnp
from jax import lax
from jax.experimental import pallas as pl
from jax.experimental.pallas import tpu as pltpu
from jax.sharding import PartitionSpec as P

K = 128
TILE = 128
LAYERS = 4
D_MAX = 32
REACH = LAYERS * D_MAX
MESH = pl.DeviceIdType.MESH
F32 = jnp.float32
BF16 = jnp.bfloat16


def kernel(
    count,
    groups,
    y_hbm,
    mask_hbm,
    f_hbm,
    m_hbm,
    v_hbm,
    b_hbm,
    dil_hbm,
    w_hbm,
    cb_hbm,
    f_end,
    m_end,
    v_end,
    b_end,
    f_out,
    m_out,
    v_out,
    b_out,
    y_buf,
    mask_in,
    mask_ref,
    dil_ref,
    f_own,
    m_own,
    v_own,
    b_own,
    w_buf,
    cb_buf,
    f_buf,
    x_buf,
    xt_buf,
    rim,
    g_own,
    g_give,
    g_take,
    y_sum_out,
    y_sum_in,
    z_sum_out,
    z_sum_in,
    gx,
    gx_out,
    gx_in,
    h_buf,
    load_sem,
    z_send,
    z_recv,
    y_send,
    y_recv,
    pair_send,
    pair_recv,
    x_send,
    x_recv,
    rim_sem,
    give_send,
    give_recv,
    y_sum_send,
    y_sum_recv,
    z_sum_send,
    z_sum_recv,
    gx_send,
    gx_recv,
):
    side = count // 4
    rows = f_own.shape[0]
    part, width = b_own.shape
    total_time = width * count
    total_series = rows * count * groups

    series = lax.axis_index("series")
    tm = lax.axis_index("tm")
    core = lax.rem(tm, 2)
    twin = 1 - core
    y_at = lax.rem(tm // 2, 2)
    over = 1 - y_at
    z_at = tm // 4

    def column(step):
        return lax.rem(z_at + side + step, side)

    def member(z, y, which):
        return (series, 4 * z + 2 * y + which)

    sibling = member(z_at, y_at, twin)
    across = member(z_at, over, core)
    ahead = [member(column(step), y_at, core) for step in range(side)]
    behind = [member(column(-step), y_at, core) for step in range(side)]
    following = (series, lax.rem(tm + 1, count))
    preceding = (series, lax.rem(tm + count - 1, count))

    loads = [
        pltpu.make_async_copy(source, target, load_sem.at[index])
        for index, (source, target) in enumerate(
            (
                (b_hbm, b_own),
                (f_hbm, f_own),
                (y_hbm, y_buf),
                (w_hbm, w_buf),
                (cb_hbm, cb_buf),
                (m_hbm, m_own),
                (v_hbm, v_own),
                (mask_hbm, mask_in),
                (dil_hbm, dil_ref),
            )
        )
    ]
    for load in loads:
        load.start()

    barrier = pltpu.get_barrier_semaphore()
    others = [(lax.rem(series + step, groups), tm) for step in range(1, groups)]
    greeted = ahead[1:] + [across, sibling, following, preceding] + others
    for device in greeted:
        pl.semaphore_signal(barrier, inc=1, device_id=device, device_id_type=MESH)
    loads[1].wait()
    f_buf[z_at, y_at, core] = f_own[...].astype(BF16)
    loads[0].wait()
    x_buf[series] = b_own[...].astype(BF16)
    gx[...] = jnp.zeros_like(gx)
    pl.semaphore_wait(barrier, len(greeted))

    def remote(source, target, send, recv, device):
        return pltpu.make_async_remote_copy(
            src_ref=source,
            dst_ref=target,
            send_sem=send,
            recv_sem=recv,
            device_id=device,
            device_id_type=MESH,
        )

    pending = []

    def send(copy):
        copy.start()
        pending.append(copy)

    def same(ref, sends, recvs, index, device):
        return remote(ref, ref, sends.at[index], recvs.at[index], device)

    def z_arrival(step):
        ref = f_buf.at[column(-step), y_at, core]
        same(ref, z_send, z_recv, step - 1, ahead[step]).wait_recv()
        pass_on(step)

    def pass_on(step):
        ref = f_buf.at[column(-step), y_at, core]
        send(same(ref, y_send, y_recv, step, across))
        send(same(ref, pair_send, pair_recv, (step, 0), sibling))

    def y_arrival(step):
        ref = f_buf.at[column(-step), over, core]
        same(ref, y_send, y_recv, step, across).wait_recv()
        send(same(ref, pair_send, pair_recv, (step, 1), sibling))

    for step in range(1, side):
        ref = f_buf.at[z_at, y_at, core]
        send(same(ref, z_send, z_recv, step - 1, ahead[step]))
        if step == 1:
            pass_on(0)
    for step in range(1, groups):
        send(
            remote(
                x_buf.at[series],
                x_buf.at[series],
                x_send.at[step - 1],
                x_recv.at[step - 1],
                others[step - 1],
            )
        )
    for step in range(1, groups):
        origin = lax.rem(series + groups - step, groups)
        remote(
            x_buf.at[origin],
            x_buf.at[origin],
            x_send.at[step - 1],
            x_recv.at[step - 1],
            others[step - 1],
        ).wait_recv()
    rim_copy = remote(
        x_buf.at[:, :, pl.ds(width - REACH, REACH)],
        rim,
        rim_sem.at[0],
        rim_sem.at[1],
        following,
    )

    @pl.when(tm < count - 1)
    def _():
        rim_copy.start()

    x_now = x_buf[...].reshape(K, width)
    xt_buf[...] = x_now.astype(F32).T.astype(BF16)
    loads[2].wait()
    loads[7].wait()
    mask_ref[...] = mask_in[...].astype(F32).T

    band = min(rows, TILE)

    def compute(z, y, which):
        block = 4 * z + 2 * y + which
        f_now = f_buf[z, y, which]
        x_full = x_buf[...].reshape(K, width)
        pred = jnp.dot(f_now, x_full, preferred_element_type=F32)
        parts = []
        for index in range(rows // band):
            start = pl.multiple_of(block * rows + index * band, band)
            tile_row = start // TILE
            y_now = y_buf[pl.ds(start, band), :].astype(F32)
            flags = mask_ref[pl.ds(tile_row, 1), :]
            seen = jnp.concatenate(
                [
                    jnp.broadcast_to(flags[:, column : column + 1], (1, TILE))
                    for column in range(width // TILE)
                ],
                axis=1,
            )
            inner = pred[index * band : (index + 1) * band]
            parts.append((seen * (y_now - inner)).astype(BF16))
        rb = jnp.concatenate(parts, axis=0) if len(parts) > 1 else parts[0]
        gx[...] += lax.dot_general(
            f_now, rb, (((0,), (0,)), ((), ())), preferred_element_type=F32
        )
        return jnp.dot(rb, xt_buf[...], preferred_element_type=F32)

    def own_block(step, row):
        g_own[step, row] = compute(column(-step), over if row else y_at, core)

    def give_copy(step, row):
        index = (step, row)
        return remote(
            g_give.at[index], g_take.at[index], give_send.at[index], give_recv.at[index], sibling
        )

    def twin_block(step, row):
        z, y = column(-step), over if row else y_at
        same(f_buf.at[z, y, twin], pair_send, pair_recv, (step, row), sibling).wait_recv()
        g_give[step, row] = compute(z, y, twin).astype(BF16)
        send(give_copy(step, row))

    def pair_total(step, row):
        give_copy(step, row).wait_recv()
        return g_own[step, row] + g_take[step, row].astype(F32)

    def y_sum_copy(step):
        return remote(
            y_sum_out.at[step],
            y_sum_in.at[step],
            y_sum_send.at[step],
            y_sum_recv.at[step],
            across,
        )

    def y_send_sum(step):
        y_sum_out[step] = pair_total(step, 1).astype(BF16)
        send(y_sum_copy(step))

    def chip_total(step):
        total = pair_total(step, 0)
        y_sum_copy(step).wait_recv()
        return total + y_sum_in[step].astype(F32)

    def z_sum_copy(step):
        return remote(
            z_sum_out.at[step - 1],
            z_sum_in.at[step - 1],
            z_sum_send.at[step - 1],
            z_sum_recv.at[step - 1],
            behind[step],
        )

    def z_send_sum(step):
        z_sum_out[step - 1] = chip_total(step).astype(BF16)
        send(z_sum_copy(step))

    own_block(0, 0)
    z_arrival(1)
    y_arrival(0)
    twin_block(0, 0)
    if side > 2:
        z_arrival(2)
    own_block(0, 1)
    if side > 3:
        z_arrival(3)
    y_arrival(1)
    twin_block(0, 1)
    for step in range(1, side):
        if step + 3 < side:
            z_arrival(step + 3)
        if step + 1 < side:
            y_arrival(step + 1)
        twin_block(step, 1)
        if step == 1:
            y_send_sum(0)
        own_block(step, 1)
        if step > 1:
            z_send_sum(step - 1)
        twin_block(step, 0)
        y_send_sum(step)
        own_block(step, 0)

    for step in range(1, groups):
        target = lax.rem(series + step, groups)
        rows_of = pl.ds(pl.multiple_of(target * part, part), part)
        gx_out[step - 1] = gx[rows_of, :].astype(BF16)
        send(
            remote(
                gx_out.at[step - 1],
                gx_in.at[step - 1],
                gx_send.at[step - 1],
                gx_recv.at[step - 1],
                others[step - 1],
            )
        )

    span = width + REACH
    @pl.when(tm > 0)
    def _():
        rim_copy.wait_recv()

    loads[3].wait()
    loads[4].wait()
    loads[8].wait()
    places = tm * width - REACH + lax.broadcasted_iota(jnp.int32, (K, span), 1)
    inside = places >= 0
    hidden = jnp.concatenate([rim[...].reshape(K, REACH), x_now], axis=1).astype(F32)
    hidden = jnp.where(inside, hidden, 0.0)

    def conv_layer(hidden, layer):
        hb = hidden.astype(BF16)
        past = pltpu.roll(hb.astype(F32), dil_ref[layer], 1).astype(BF16)
        z_val = jnp.dot(w_buf[layer, 0], past, preferred_element_type=F32)
        z_val = z_val + jnp.dot(w_buf[layer, 1], hb, preferred_element_type=F32)
        z_val = z_val + cb_buf[layer][:, None]
        return jnp.where(inside, hidden + jnp.maximum(z_val, 0.0), 0.0)

    for layer in range(LAYERS):
        if layer == LAYERS // 2:
            z_send_sum(side - 1)
        hidden = conv_layer(hidden, layer)
    h_buf[...] = hidden[:, REACH:]

    own_rows = pl.ds(pl.multiple_of(series * part, part), part)
    grad_x = gx[own_rows, :]
    for step in range(1, groups):
        remote(
            gx_out.at[step - 1],
            gx_in.at[step - 1],
            gx_send.at[step - 1],
            gx_recv.at[step - 1],
            others[step - 1],
        ).wait_recv()
        grad_x = grad_x + gx_in[step - 1].astype(F32)
    grad_x = -grad_x * math.sqrt(K / total_series)
    basis = b_own[...]
    b_out[...] = basis - 0.5 * (grad_x + (basis - h_buf[own_rows, :]))
    stores = [
        pltpu.make_async_copy(source, target, load_sem.at[len(loads) + index])
        for index, (source, target) in enumerate(
            ((f_out, f_end), (m_out, m_end), (v_out, v_end), (b_out, b_end))
        )
    ]
    stores[3].start()

    loads[5].wait()
    loads[6].wait()
    scale_f = 1.0 / math.sqrt(total_time)
    value = chip_total(0)
    for step in range(1, side):
        z_sum_copy(step).wait_recv()
        value = value + z_sum_in[step - 1].astype(F32)
    grad_f = -value * scale_f
    m_new = 0.9 * m_own[...] + 0.1 * grad_f
    v_new = 0.999 * v_own[...] + 0.001 * grad_f * grad_f
    m_hat = m_new / (1.0 - 0.9**10)
    v_hat = v_new / (1.0 - 0.999**10)
    f_out[...] = f_own[...] - 0.01 * m_hat / (jnp.sqrt(v_hat) + 1e-08)
    m_out[...] = m_new
    v_out[...] = v_new
    for store in stores[:3]:
        store.start()

    for copy in pending:
        copy.wait_send()

    @pl.when(tm < count - 1)
    def _():
        rim_copy.wait_send()

    for store in stores:
        store.wait()


def hand_out(*refs):
    sources, targets, held, sem = refs[:4], refs[4:8], refs[8:12], refs[12]
    loads = [pltpu.make_async_copy(sources[i], held[i], sem.at[i]) for i in range(4)]
    stores = [pltpu.make_async_copy(held[i], targets[i], sem.at[4 + i]) for i in range(4)]
    for load in loads:
        load.start()
    for load, store in zip(loads, stores):
        load.wait()
        store.start()
    for store in stores:
        store.wait()


def on_device(count, groups, y_obs, tile_mask, factors, adam_m, adam_v, basis, dilations, conv_w, conv_b):
    rows = factors.shape[0]
    part, width = basis.shape
    side = count // 4
    dma = pltpu.SemaphoreType.DMA
    hbm = pl.BlockSpec(memory_space=pltpu.HBM)
    work = y_obs.shape[0] * width * K * 6
    results = pl.pallas_call(
        functools.partial(kernel, count, groups),
        out_shape=(
            jax.ShapeDtypeStruct(factors.shape, F32),
            jax.ShapeDtypeStruct(factors.shape, F32),
            jax.ShapeDtypeStruct(factors.shape, F32),
            jax.ShapeDtypeStruct(basis.shape, F32),
        ),
        in_specs=[hbm] * 9,
        out_specs=(hbm,) * 4,
        scratch_shapes=[
            pltpu.VMEM(factors.shape, F32),
            pltpu.VMEM(factors.shape, F32),
            pltpu.VMEM(factors.shape, F32),
            pltpu.VMEM(basis.shape, F32),
            pltpu.VMEM(y_obs.shape, BF16),
            pltpu.VMEM(tile_mask.shape[::-1], jnp.int32),
            pltpu.VMEM(tile_mask.shape, F32),
            pltpu.SMEM(dilations.shape, jnp.int32),
            pltpu.VMEM(factors.shape, F32),
            pltpu.VMEM(factors.shape, F32),
            pltpu.VMEM(factors.shape, F32),
            pltpu.VMEM(basis.shape, F32),
            pltpu.VMEM(conv_w.shape, BF16),
            pltpu.VMEM(conv_b.shape, F32),
            pltpu.VMEM((side, 2, 2, rows, K), BF16),
            pltpu.VMEM((groups, part, width), BF16),
            pltpu.VMEM((width, K), BF16),
            pltpu.VMEM((groups, part, REACH), BF16),
            pltpu.VMEM((side, 2, rows, K), F32),
            pltpu.VMEM((side, 2, rows, K), BF16),
            pltpu.VMEM((side, 2, rows, K), BF16),
            pltpu.VMEM((side, rows, K), BF16),
            pltpu.VMEM((side, rows, K), BF16),
            pltpu.VMEM((side - 1, rows, K), BF16),
            pltpu.VMEM((side - 1, rows, K), BF16),
            pltpu.VMEM((K, width), F32),
            pltpu.VMEM((max(groups - 1, 1), part, width), BF16),
            pltpu.VMEM((max(groups - 1, 1), part, width), BF16),
            pltpu.VMEM((K, width), F32),
            dma((13,)),
            dma((side - 1,)),
            dma((side - 1,)),
            dma((side,)),
            dma((side,)),
            dma((side, 2)),
            dma((side, 2)),
            dma((max(groups - 1, 1),)),
            dma((max(groups - 1, 1),)),
            dma((2,)),
            dma((side, 2)),
            dma((side, 2)),
            dma((side,)),
            dma((side,)),
            dma((side - 1,)),
            dma((side - 1,)),
            dma((max(groups - 1, 1),)),
            dma((max(groups - 1, 1),)),
        ],
        compiler_params=pltpu.CompilerParams(
            collective_id=0, has_side_effects=True, vmem_limit_bytes=60 * 2**20
        ),
        cost_estimate=pl.CostEstimate(
            flops=work, bytes_accessed=2 * y_obs.size, transcendentals=factors.size
        ),
    )(y_obs, tile_mask.T, factors, adam_m, adam_v, basis, dilations, conv_w, conv_b)
    return pl.pallas_call(
        hand_out,
        out_shape=tuple(jax.ShapeDtypeStruct(result.shape, F32) for result in results),
        in_specs=[hbm] * 4,
        out_specs=(hbm,) * 4,
        scratch_shapes=[pltpu.VMEM(result.shape, F32) for result in results] + [dma((8,))],
        compiler_params=pltpu.CompilerParams(vmem_limit_bytes=60 * 2**20),
    )(*results)


def solution(mesh):
    return jax.shard_map(
        functools.partial(on_device, mesh.shape["tm"], mesh.shape["series"]),
        mesh=mesh,
        in_specs=(
            P("series", "tm"),
            P("series", "tm"),
            P(("series", "tm"), None),
            P(("series", "tm"), None),
            P(("series", "tm"), None),
            P("series", "tm"),
            P(),
            P(),
            P(),
        ),
        out_specs=(
            P(("series", "tm"), None),
            P(("series", "tm"), None),
            P(("series", "tm"), None),
            P("series", "tm"),
        ),
        check_vma=False,
    )
```

profile of v0, /device:TPU:0, one launch (start us, length us, event | category | flops | bytes accessed | tf_op | source)
XLA Modules:
  0.0 36.2 jit_solution(9096175895662793206)
XLA Ops:
  0.6 33.7 %shard_map.120 = (f32[256,128]{1,0:T(8,128)}, f32[256,128]{1,0:T(8,128)}, f32[256,128]{1,0:T(8,128)}, f32[64,512]{1,0:T(8,128)}) custom-call(bf16[4096,512]{1,0:T(8,128)(2,1)} %y_hbm.1, s32[4,32]{1,0:T(4,128)} %bitcast.1, f32[256,128]{1,0:T(8,128)} %f_hbm.1, f32[256,128]{1,0:T(8,128)} %m_hbm.1, f32[256,128]{1,0:T(8,128)} %v_hbm.1, f32[64,512]{1,0:T(8,128)} %b_hbm.1, ...), custom_call_target="tpu_custom_call" | custom-call | flops 1610612736 | bytes 4194304 | tf_op jit(solution)/shard_map/pallas_call | solution.py:435
  34.4 1.8 %shard_map.121 = (f32[256,128]{1,0:T(8,128)}, f32[256,128]{1,0:T(8,128)}, f32[256,128]{1,0:T(8,128)}, f32[64,512]{1,0:T(8,128)}) custom-call(f32[256,128]{1,0:T(8,128)} %get-tuple-element.8.refs_0_, f32[256,128]{1,0:T(8,128)} %get-tuple-element.9.refs_1_, f32[256,128]{1,0:T(8,128)} %get-tuple-element.10.refs_2_, f32[64,512]{1,0:T(8,128)} %get-tuple-element.11.refs_3_), custom_call_target="tpu_custom_call" | custom-call | tf_op jit(solution)/shard_map/pallas_call | solution.py:501
where the time goes:
time: 36.3 us; the launch traced here: 36.2 us
  Pallas kernels  35.6 us (98%)
  between operations  0.64 us (2%)
    pallas_call x1, Pallas kernels, on_device(): pl.pallas_call(functools.partial(kernel, count, groups), out_shape=(jax.S...  33.7 us
    pallas_call x1, Pallas kernels, on_device(): pl.pallas_call(hand_out, out_shape=tuple((jax.ShapeDtypeStruct(result.sha...  1.82 us

commit v1 on v0

--- a/solution.py
+++ b/solution.py
@@ -52,6 +52,7 @@
     x_buf,
     xt_buf,
     rim,
+    g_both,
     g_own,
     g_give,
     g_take,
@@ -130,15 +131,20 @@
 
     barrier = pltpu.get_barrier_semaphore()
     others = [(lax.rem(series + step, groups), tm) for step in range(1, groups)]
-    greeted = ahead[1:] + [across, sibling, following, preceding] + others
+    greeted = ahead[1:] + [across, sibling] + others
     for device in greeted:
         pl.semaphore_signal(barrier, inc=1, device_id=device, device_id_type=MESH)
+
+    @pl.when(tm > 0)
+    def _():
+        pl.semaphore_signal(barrier, inc=1, device_id=preceding, device_id_type=MESH)
+
     loads[1].wait()
     f_buf[z_at, y_at, core] = f_own[...].astype(BF16)
     loads[0].wait()
     x_buf[series] = b_own[...].astype(BF16)
     gx[...] = jnp.zeros_like(gx)
-    pl.semaphore_wait(barrier, len(greeted))
+    pl.semaphore_wait(barrier, len(greeted) + jnp.where(tm < count - 1, 1, 0))
 
     def remote(source, target, send, recv, device):
         return pltpu.make_async_remote_copy(
@@ -174,11 +180,6 @@
         same(ref, y_send, y_recv, step, across).wait_recv()
         send(same(ref, pair_send, pair_recv, (step, 1), sibling))
 
-    for step in range(1, side):
-        ref = f_buf.at[z_at, y_at, core]
-        send(same(ref, z_send, z_recv, step - 1, ahead[step]))
-        if step == 1:
-            pass_on(0)
     for step in range(1, groups):
         send(
             remote(
@@ -189,6 +190,12 @@
                 others[step - 1],
             )
         )
+    for step in range(1, side):
+        ref = f_buf.at[z_at, y_at, core]
+        send(same(ref, z_send, z_recv, step - 1, ahead[step]))
+        if step == 1:
+            pass_on(0)
+
     for step in range(1, groups):
         origin = lax.rem(series + groups - step, groups)
         remote(
@@ -216,36 +223,32 @@
     loads[7].wait()
     mask_ref[...] = mask_in[...].astype(F32).T
 
-    band = min(rows, TILE)
-
-    def compute(z, y, which):
-        block = 4 * z + 2 * y + which
-        f_now = f_buf[z, y, which]
+    band = min(2 * rows, 2 * TILE)
+
+    def compute(z, y):
+        first = (4 * z + 2 * y) * rows
+        f_now = f_buf[z, y].reshape(2 * rows, K)
         x_full = x_buf[...].reshape(K, width)
-        pred = jnp.dot(f_now, x_full, preferred_element_type=F32)
         parts = []
-        for index in range(rows // band):
-            start = pl.multiple_of(block * rows + index * band, band)
-            tile_row = start // TILE
-            y_now = y_buf[pl.ds(start, band), :].astype(F32)
-            flags = mask_ref[pl.ds(tile_row, 1), :]
-            seen = jnp.concatenate(
-                [
-                    jnp.broadcast_to(flags[:, column : column + 1], (1, TILE))
-                    for column in range(width // TILE)
-                ],
-                axis=1,
-            )
-            inner = pred[index * band : (index + 1) * band]
-            parts.append((seen * (y_now - inner)).astype(BF16))
+        for start in range(0, 2 * rows, band):
+            pred = jnp.dot(f_now[start : start + band], x_full, preferred_element_type=F32)
+            for inner in range(0, band, TILE):
+                at = pl.multiple_of(first + start + inner, TILE)
+                y_now = y_buf[pl.ds(at, TILE), :].astype(F32)
+                flags = mask_ref[pl.ds(at // TILE, 1), :]
+                seen = jnp.concatenate(
+                    [
+                        jnp.broadcast_to(flags[:, column : column + 1], (1, TILE))
+                        for column in range(width // TILE)
+                    ],
+                    axis=1,
+                )
+                parts.append((seen * (y_now - pred[inner : inner + TILE])).astype(BF16))
         rb = jnp.concatenate(parts, axis=0) if len(parts) > 1 else parts[0]
         gx[...] += lax.dot_general(
             f_now, rb, (((0,), (0,)), ((), ())), preferred_element_type=F32
         )
         return jnp.dot(rb, xt_buf[...], preferred_element_type=F32)
-
-    def own_block(step, row):
-        g_own[step, row] = compute(column(-step), over if row else y_at, core)
 
     def give_copy(step, row):
         index = (step, row)
@@ -253,11 +256,13 @@
             g_give.at[index], g_take.at[index], give_send.at[index], give_recv.at[index], sibling
         )
 
-    def twin_block(step, row):
+    def block(step, row):
         z, y = column(-step), over if row else y_at
         same(f_buf.at[z, y, twin], pair_send, pair_recv, (step, row), sibling).wait_recv()
-        g_give[step, row] = compute(z, y, twin).astype(BF16)
+        g_both[...] = compute(z, y).reshape(2, rows, K)
+        g_give[step, row] = g_both[twin].astype(BF16)
         send(give_copy(step, row))
+        g_own[step, row] = g_both[core]
 
     def pair_total(step, row):
         give_copy(step, row).wait_recv()
@@ -294,31 +299,27 @@
         z_sum_out[step - 1] = chip_total(step).astype(BF16)
         send(z_sum_copy(step))
 
-    own_block(0, 0)
+    block(0, 0)
     z_arrival(1)
     y_arrival(0)
-    twin_block(0, 0)
     if side > 2:
         z_arrival(2)
-    own_block(0, 1)
+    block(0, 1)
     if side > 3:
         z_arrival(3)
     y_arrival(1)
-    twin_block(0, 1)
     for step in range(1, side):
         if step + 3 < side:
             z_arrival(step + 3)
         if step + 1 < side:
             y_arrival(step + 1)
-        twin_block(step, 1)
+        block(step, 1)
         if step == 1:
             y_send_sum(0)
-        own_block(step, 1)
-        if step > 1:
+        else:
             z_send_sum(step - 1)
-        twin_block(step, 0)
+        block(step, 0)
         y_send_sum(step)
-        own_block(step, 0)
 
     for step in range(1, groups):
         target = lax.rem(series + step, groups)
@@ -461,6 +462,7 @@
             pltpu.VMEM((groups, part, width), BF16),
             pltpu.VMEM((width, K), BF16),
             pltpu.VMEM((groups, part, REACH), BF16),
+            pltpu.VMEM((2, rows, K), F32),
             pltpu.VMEM((side, 2, rows, K), F32),
             pltpu.VMEM((side, 2, rows, K), BF16),
             pltpu.VMEM((side, 2, rows, K), BF16),

time: 36.3 us -> 37.4 us (1.030)
  Pallas kernels: 35.6 us -> 36.6 us
    pallas_call x1, Pallas kernels: 33.7 us -> 34.8 us  [on_device(): pl.pallas_call(functools.partial(kernel, count, groups), out_shape=(jax.S...]
where the time goes in v1:
time: 37.4 us; the launch traced here: 37.3 us
  Pallas kernels  36.6 us (98%)
  between operations  0.64 us (2%)
    pallas_call x1, Pallas kernels, on_device(): pl.pallas_call(functools.partial(kernel, count, groups), out_shape=(jax.S...  34.8 us
    pallas_call x1, Pallas kernels, on_device(): pl.pallas_call(hand_out, out_shape=tuple((jax.ShapeDtypeStruct(result.sha...  1.82 us

profile of v1, /device:TPU:0, one launch (start us, length us, event | category | flops | bytes accessed | tf_op | source)
XLA Modules:
  0.0 37.3 jit_solution(17151387448075791872)
XLA Ops:
  0.6 34.8 %shard_map.120 = (f32[256,128]{1,0:T(8,128)}, f32[256,128]{1,0:T(8,128)}, f32[256,128]{1,0:T(8,128)}, f32[64,512]{1,0:T(8,128)}) custom-call(bf16[4096,512]{1,0:T(8,128)(2,1)} %y_hbm.1, s32[4,32]{1,0:T(4,128)} %bitcast.1, f32[256,128]{1,0:T(8,128)} %f_hbm.1, f32[256,128]{1,0:T(8,128)} %m_hbm.1, f32[256,128]{1,0:T(8,128)} %v_hbm.1, f32[64,512]{1,0:T(8,128)} %b_hbm.1, ...), custom_call_target="tpu_custom_call" | custom-call | flops 1610612736 | bytes 4194304 | tf_op jit(solution)/shard_map/pallas_call | solution.py:436
  35.4 1.8 %shard_map.121 = (f32[256,128]{1,0:T(8,128)}, f32[256,128]{1,0:T(8,128)}, f32[256,128]{1,0:T(8,128)}, f32[64,512]{1,0:T(8,128)}) custom-call(f32[256,128]{1,0:T(8,128)} %get-tuple-element.8.refs_0_, f32[256,128]{1,0:T(8,128)} %get-tuple-element.9.refs_1_, f32[256,128]{1,0:T(8,128)} %get-tuple-element.10.refs_2_, f32[64,512]{1,0:T(8,128)} %get-tuple-element.11.refs_3_), custom_call_target="tpu_custom_call" | custom-call | tf_op jit(solution)/shard_map/pallas_call | solution.py:503

commit v2 on v1

--- a/solution.py
+++ b/solution.py
@@ -304,22 +304,18 @@
     y_arrival(0)
     if side > 2:
         z_arrival(2)
-    block(0, 1)
-    if side > 3:
-        z_arrival(3)
-    y_arrival(1)
     for step in range(1, side):
-        if step + 3 < side:
-            z_arrival(step + 3)
-        if step + 1 < side:
-            y_arrival(step + 1)
+        block(step, 0)
+        if step + 2 < side:
+            z_arrival(step + 2)
+        y_arrival(step)
+    order = list(range(1, side)) + [0]
+    for turn, step in enumerate(order):
         block(step, 1)
-        if step == 1:
-            y_send_sum(0)
-        else:
-            z_send_sum(step - 1)
-        block(step, 0)
-        y_send_sum(step)
+        if turn >= 1:
+            y_send_sum(order[turn - 1])
+        if turn >= 2:
+            z_send_sum(order[turn - 2])
 
     for step in range(1, groups):
         target = lax.rem(series + step, groups)
@@ -357,7 +353,9 @@
         return jnp.where(inside, hidden + jnp.maximum(z_val, 0.0), 0.0)
 
     for layer in range(LAYERS):
-        if layer == LAYERS // 2:
+        if layer == 1:
+            y_send_sum(0)
+        if layer == 2:
             z_send_sum(side - 1)
         hidden = conv_layer(hidden, layer)
     h_buf[...] = hidden[:, REACH:]

time: 37.4 us -> 35.3 us (0.944)
  Pallas kernels: 36.6 us -> 34.5 us
    pallas_call x1, Pallas kernels: 34.8 us -> 32.7 us  [on_device(): pl.pallas_call(functools.partial(kernel, count, groups), out_shape=(jax.S...]
where the time goes in v2:
time: 35.3 us; the launch traced here: 35.1 us
  Pallas kernels  34.5 us (98%)
  between operations  0.64 us (2%)
    pallas_call x1, Pallas kernels, on_device(): pl.pallas_call(functools.partial(kernel, count, groups), out_shape=(jax.S...  32.7 us
    pallas_call x1, Pallas kernels, on_device(): pl.pallas_call(hand_out, out_shape=tuple((jax.ShapeDtypeStruct(result.sha...  1.82 us

profile of v2, /device:TPU:0, one launch (start us, length us, event | category | flops | bytes accessed | tf_op | source)
XLA Modules:
  0.0 35.1 jit_solution(1000237434589107507)
XLA Ops:
  0.6 32.7 %shard_map.120 = (f32[256,128]{1,0:T(8,128)}, f32[256,128]{1,0:T(8,128)}, f32[256,128]{1,0:T(8,128)}, f32[64,512]{1,0:T(8,128)}) custom-call(bf16[4096,512]{1,0:T(8,128)(2,1)} %y_hbm.1, s32[4,32]{1,0:T(4,128)} %bitcast.1, f32[256,128]{1,0:T(8,128)} %f_hbm.1, f32[256,128]{1,0:T(8,128)} %m_hbm.1, f32[256,128]{1,0:T(8,128)} %v_hbm.1, f32[64,512]{1,0:T(8,128)} %b_hbm.1, ...), custom_call_target="tpu_custom_call" | custom-call | flops 1610612736 | bytes 4194304 | tf_op jit(solution)/shard_map/pallas_call | solution.py:434
  33.3 1.8 %shard_map.121 = (f32[256,128]{1,0:T(8,128)}, f32[256,128]{1,0:T(8,128)}, f32[256,128]{1,0:T(8,128)}, f32[64,512]{1,0:T(8,128)}) custom-call(f32[256,128]{1,0:T(8,128)} %get-tuple-element.8.refs_0_, f32[256,128]{1,0:T(8,128)} %get-tuple-element.9.refs_1_, f32[256,128]{1,0:T(8,128)} %get-tuple-element.10.refs_2_, f32[64,512]{1,0:T(8,128)} %get-tuple-element.11.refs_3_), custom_call_target="tpu_custom_call" | custom-call | tf_op jit(solution)/shard_map/pallas_call | solution.py:501

commit v3 on v2

--- a/solution.py
+++ b/solution.py
@@ -106,7 +106,6 @@
     sibling = member(z_at, y_at, twin)
     across = member(z_at, over, core)
     ahead = [member(column(step), y_at, core) for step in range(side)]
-    behind = [member(column(-step), y_at, core) for step in range(side)]
     following = (series, lax.rem(tm + 1, count))
     preceding = (series, lax.rem(tm + count - 1, count))
 
@@ -167,18 +166,18 @@
 
     def z_arrival(step):
         ref = f_buf.at[column(-step), y_at, core]
-        same(ref, z_send, z_recv, step - 1, ahead[step]).wait_recv()
+        same(ref, z_send, z_recv, step - 1, across).wait_recv()
         pass_on(step)
 
     def pass_on(step):
         ref = f_buf.at[column(-step), y_at, core]
-        send(same(ref, y_send, y_recv, step, across))
-        send(same(ref, pair_send, pair_recv, (step, 0), sibling))
+        same(ref, y_send, y_recv, step, across).start()
+        same(ref, pair_send, pair_recv, (step, 0), sibling).start()
 
     def y_arrival(step):
         ref = f_buf.at[column(-step), over, core]
         same(ref, y_send, y_recv, step, across).wait_recv()
-        send(same(ref, pair_send, pair_recv, (step, 1), sibling))
+        same(ref, pair_send, pair_recv, (step, 1), sibling).start()
 
     for step in range(1, groups):
         send(
@@ -257,11 +256,11 @@
         )
 
     def block(step, row):
-        z, y = column(-step), over if row else y_at
+        z, y = column(-step), y_at + row * (over - y_at)
         same(f_buf.at[z, y, twin], pair_send, pair_recv, (step, row), sibling).wait_recv()
         g_both[...] = compute(z, y).reshape(2, rows, K)
         g_give[step, row] = g_both[twin].astype(BF16)
-        send(give_copy(step, row))
+        give_copy(step, row).start()
         g_own[step, row] = g_both[core]
 
     def pair_total(step, row):
@@ -279,7 +278,7 @@
 
     def y_send_sum(step):
         y_sum_out[step] = pair_total(step, 1).astype(BF16)
-        send(y_sum_copy(step))
+        y_sum_copy(step).start()
 
     def chip_total(step):
         total = pair_total(step, 0)
@@ -292,30 +291,37 @@
             z_sum_in.at[step - 1],
             z_sum_send.at[step - 1],
             z_sum_recv.at[step - 1],
-            behind[step],
+            member(column(-step), y_at, core),
         )
 
     def z_send_sum(step):
         z_sum_out[step - 1] = chip_total(step).astype(BF16)
-        send(z_sum_copy(step))
-
-    block(0, 0)
-    z_arrival(1)
-    y_arrival(0)
-    if side > 2:
-        z_arrival(2)
-    for step in range(1, side):
-        block(step, 0)
-        if step + 2 < side:
-            z_arrival(step + 2)
-        y_arrival(step)
-    order = list(range(1, side)) + [0]
-    for turn, step in enumerate(order):
-        block(step, 1)
-        if turn >= 1:
-            y_send_sum(order[turn - 1])
-        if turn >= 2:
-            z_send_sum(order[turn - 2])
+        z_sum_copy(step).start()
+
+    @pl.loop(0, 2 * side)
+    def _(turn):
+        row = turn // side
+        block(lax.rem(turn + row, side), row)
+
+        @pl.when(turn == 0)
+        def _():
+            z_arrival(1)
+
+        @pl.when(turn + 2 < side)
+        def _():
+            z_arrival(turn + 2)
+
+        @pl.when(turn < side)
+        def _():
+            y_arrival(turn)
+
+        @pl.when(turn > side)
+        def _():
+            y_send_sum(turn - side)
+
+        @pl.when(turn > side + 1)
+        def _():
+            z_send_sum(turn - side - 1)
 
     for step in range(1, groups):
         target = lax.rem(series + step, groups)
@@ -402,6 +408,21 @@
 
     for copy in pending:
         copy.wait_send()
+
+    @pl.loop(0, side)
+    def _(step):
+        own = f_buf.at[column(-step), y_at, core]
+        other = f_buf.at[column(-step), over, core]
+        same(own, y_send, y_recv, step, across).wait_send()
+        same(own, pair_send, pair_recv, (step, 0), sibling).wait_send()
+        same(other, pair_send, pair_recv, (step, 1), sibling).wait_send()
+        give_copy(step, 0).wait_send()
+        give_copy(step, 1).wait_send()
+        y_sum_copy(step).wait_send()
+
+        @pl.when(step > 0)
+        def _():
+            z_sum_copy(step).wait_send()
 
     @pl.when(tm < count - 1)
     def _():

time: 35.3 us -> 35 us (level)
  no operation moved by 1% of the time
where the time goes in v3:
time: 35 us; the launch traced here: 34.8 us
  Pallas kernels  34.2 us (98%)
  between operations  0.64 us (2%)
    pallas_call x1, Pallas kernels, on_device(): pl.pallas_call(functools.partial(kernel, count, groups), out_shape=(jax.S...  32.4 us
    pallas_call x1, Pallas kernels, on_device(): pl.pallas_call(hand_out, out_shape=tuple((jax.ShapeDtypeStruct(result.sha...  1.82 us

profile of v3, /device:TPU:0, one launch (start us, length us, event | category | flops | bytes accessed | tf_op | source)
XLA Modules:
  0.0 34.8 jit_solution(4999195193608074515)
XLA Ops:
  0.6 32.4 %shard_map.120 = (f32[256,128]{1,0:T(8,128)}, f32[256,128]{1,0:T(8,128)}, f32[256,128]{1,0:T(8,128)}, f32[64,512]{1,0:T(8,128)}) custom-call(bf16[4096,512]{1,0:T(8,128)(2,1)} %y_hbm.1, s32[4,32]{1,0:T(4,128)} %bitcast.1, f32[256,128]{1,0:T(8,128)} %f_hbm.1, f32[256,128]{1,0:T(8,128)} %m_hbm.1, f32[256,128]{1,0:T(8,128)} %v_hbm.1, f32[64,512]{1,0:T(8,128)} %b_hbm.1, ...), custom_call_target="tpu_custom_call" | custom-call | flops 1610612736 | bytes 4194304 | tf_op jit(solution)/shard_map/pallas_call | solution.py:455
  33.0 1.8 %shard_map.121 = (f32[256,128]{1,0:T(8,128)}, f32[256,128]{1,0:T(8,128)}, f32[256,128]{1,0:T(8,128)}, f32[64,512]{1,0:T(8,128)}) custom-call(f32[256,128]{1,0:T(8,128)} %get-tuple-element.8.refs_0_, f32[256,128]{1,0:T(8,128)} %get-tuple-element.9.refs_1_, f32[256,128]{1,0:T(8,128)} %get-tuple-element.10.refs_2_, f32[64,512]{1,0:T(8,128)} %get-tuple-element.11.refs_3_), custom_call_target="tpu_custom_call" | custom-call | tf_op jit(solution)/shard_map/pallas_call | solution.py:522

commit v4 on v3

--- a/solution.py
+++ b/solution.py
@@ -125,7 +125,7 @@
             )
         )
     ]
-    for load in loads:
+    for load in loads[:2]:
         load.start()
 
     barrier = pltpu.get_barrier_semaphore()
@@ -142,6 +142,8 @@
     f_buf[z_at, y_at, core] = f_own[...].astype(BF16)
     loads[0].wait()
     x_buf[series] = b_own[...].astype(BF16)
+    for load in loads[2:]:
+        load.start()
     gx[...] = jnp.zeros_like(gx)
     pl.semaphore_wait(barrier, len(greeted) + jnp.where(tm < count - 1, 1, 0))
 

time: 35 us -> 35 us (level)
  no operation moved by 1% of the time
where the time goes in v4:
time: 35 us; the launch traced here: 34.8 us
  Pallas kernels  34.2 us (98%)
  between operations  0.64 us (2%)
    pallas_call x1, Pallas kernels, on_device(): pl.pallas_call(functools.partial(kernel, count, groups), out_shape=(jax.S...  32.3 us
    pallas_call x1, Pallas kernels, on_device(): pl.pallas_call(hand_out, out_shape=tuple((jax.ShapeDtypeStruct(result.sha...  1.82 us

profile of v4, /device:TPU:0, one launch (start us, length us, event | category | flops | bytes accessed | tf_op | source)
XLA Modules:
  0.0 34.8 jit_solution(3670791565821867313)
XLA Ops:
  0.6 32.3 %shard_map.120 = (f32[256,128]{1,0:T(8,128)}, f32[256,128]{1,0:T(8,128)}, f32[256,128]{1,0:T(8,128)}, f32[64,512]{1,0:T(8,128)}) custom-call(bf16[4096,512]{1,0:T(8,128)(2,1)} %y_hbm.1, s32[4,32]{1,0:T(4,128)} %bitcast.1, f32[256,128]{1,0:T(8,128)} %f_hbm.1, f32[256,128]{1,0:T(8,128)} %m_hbm.1, f32[256,128]{1,0:T(8,128)} %v_hbm.1, f32[64,512]{1,0:T(8,128)} %b_hbm.1, ...), custom_call_target="tpu_custom_call" | custom-call | flops 1610612736 | bytes 4194304 | tf_op jit(solution)/shard_map/pallas_call | solution.py:457
  33.0 1.8 %shard_map.121 = (f32[256,128]{1,0:T(8,128)}, f32[256,128]{1,0:T(8,128)}, f32[256,128]{1,0:T(8,128)}, f32[64,512]{1,0:T(8,128)}) custom-call(f32[256,128]{1,0:T(8,128)} %get-tuple-element.8.refs_0_, f32[256,128]{1,0:T(8,128)} %get-tuple-element.9.refs_1_, f32[256,128]{1,0:T(8,128)} %get-tuple-element.10.refs_2_, f32[64,512]{1,0:T(8,128)} %get-tuple-element.11.refs_3_), custom_call_target="tpu_custom_call" | custom-call | tf_op jit(solution)/shard_map/pallas_call | solution.py:524
